TPU v7x, 768 devices: a whole 4x8x12 slice. The times are simulated.
768 devices in a mesh: blk: 12 (over z_hi, x), team: 64 (over z_lo, y, core).
Axes of the slice: x: 4, y: 8, z: 12 (z_hi: 3, z_lo: 4; z = z_hi * 4 + z_lo), core: 2. Of those that a mesh axis runs over, the one named last changes fastest.
Arguments:
- features: bfloat16 [98304, 256], P(('blk', 'team')), may hold values from -6 to 6
- weight: bfloat16 [256, 256], replicated, may hold values from -0.375 to 0.375
- tile_values: bfloat16 [12, 64, 12, 6, 128, 128], P('blk', 'team'), may hold values from -0.046875 to 0.046875
- tile_rows: int32 [12, 64, 12, 6], P('blk', 'team'), may hold values from 0 to 15, as said below
- tile_counts: int32 [12, 64, 12], P('blk', 'team'), may hold values from 0 to 6, as said below
- grad_out: bfloat16 [24576, 256], P(('blk', 'team')), may hold values from -6 to 6
Outputs:
- layer_out: bfloat16 [24576, 256], P(('blk', 'team'))
- grad_features: bfloat16 [98304, 256], P(('blk', 'team'))
- grad_weight: float32 [256, 256], replicated
Inputs may be any that keep to these rules, and one draw needn't show every extreme that they name: `tile_rows`: within one owner's slots for one column block the row tiles are distinct. The first tile_counts[b, u, c] slots of tile_values[b, u, c] are live, the others are not part of A; some owner has 6 for some column block.
All inputs are finite; a program needn't handle non-finite values.
Results may differ from a plain program's by a relative error of at most 0.0075.
Values may be sent and summed in bfloat16 or wider, within the bound.
A program may use at most 32 MiB of HBM per device.

v0:
```python
import jax
import jax.numpy as jnp
from jax import lax
from jax.sharding import PartitionSpec as P


def from_behind(block, axis, distance):
    devices = range(lax.axis_size(axis))
    route = [((i - distance) % len(devices), i) for i in devices]
    return lax.ppermute(block, axis, route)


def body(features, weight, tile_values, tile_rows, tile_counts, grad_out):
    blocks = lax.axis_size("blk")
    here = lax.axis_index("blk")
    tiles = tile_values.reshape(tile_values.shape[2:])
    rows = tile_rows.reshape(tile_rows.shape[2:])
    counts = tile_counts.reshape(-1)
    slots = rows.shape[1]
    tile = tiles.shape[-1]
    own_rows = grad_out.shape[0]
    block_rows = own_rows * lax.axis_size("team")
    rtiles = block_rows // tile
    live = lax.iota(jnp.int32, slots)[None, :] < counts[:, None]
    live_float = live.astype(jnp.float32)
    onehot = (rows[:, :, None] == lax.iota(jnp.int32, rtiles)[None, None, :]) & live[:, :, None]
    onehot_low = onehot.astype(jnp.bfloat16)
    hidden = jnp.dot(features, weight, preferred_element_type=jnp.float32).astype(jnp.bfloat16)
    width = hidden.shape[1]

    def forward_term(acc, column, part):
        tiles_c = lax.dynamic_index_in_dim(tiles, column, 0, keepdims=False)
        rows_c = lax.dynamic_index_in_dim(rows, column, 0, keepdims=False)
        live_c = lax.dynamic_index_in_dim(live_float, column, 0, keepdims=False)
        prod = jnp.einsum("kij,jf->kif", tiles_c, part, preferred_element_type=jnp.float32)
        for slot in range(slots):
            target = rows_c[slot]
            current = lax.dynamic_index_in_dim(acc, target, 0, keepdims=False)
            acc = lax.dynamic_update_index_in_dim(
                acc, current + live_c[slot] * prod[slot], target, 0
            )
        return acc

    def backward_term(column, grads):
        tiles_c = lax.dynamic_index_in_dim(tiles, column, 0, keepdims=False)
        mask_c = lax.dynamic_index_in_dim(onehot_low, column, 0, keepdims=False)
        chosen = jnp.einsum(
            "kr,rif->kif", mask_c, grads, preferred_element_type=jnp.float32
        ).astype(jnp.bfloat16)
        return jnp.einsum("kij,kif->jf", tiles_c, chosen, preferred_element_type=jnp.float32)

    def forward_step(step, carry):
        part, acc = carry
        part = from_behind(part, "blk", 1)
        return (part, forward_term(acc, (here - step) % blocks, part))

    empty_full = jnp.zeros((rtiles, tile, width), jnp.float32)
    _, partial_value = lax.fori_loop(
        1, blocks, forward_step, (hidden, forward_term(empty_full, here, hidden))
    )
    pre = lax.psum_scatter(
        partial_value.reshape(block_rows, width), "team", scatter_dimension=0, tiled=True
    )
    sig = jax.nn.sigmoid(pre)
    layer_out = (pre * sig).astype(jnp.bfloat16)
    grad_pre = (grad_out.astype(jnp.float32) * sig * (1.0 + pre * (1.0 - sig))).astype(jnp.bfloat16)
    grads = lax.all_gather(grad_pre, "team", axis=0, tiled=True).reshape(rtiles, tile, width)

    def backward_step(step, acc):
        acc = from_behind(acc, "blk", 1)
        return acc + backward_term((here + blocks - 1 - step) % blocks, grads)

    collected = lax.fori_loop(
        1, blocks, backward_step, backward_term((here + blocks - 1) % blocks, grads)
    )
    grad_hidden = collected.astype(jnp.bfloat16)
    grad_features = jnp.dot(grad_hidden, weight.T, preferred_element_type=jnp.float32).astype(
        jnp.bfloat16
    )
    local_weight = jnp.einsum(
        "nf,ng->fg", features, grad_hidden, preferred_element_type=jnp.float32
    )
    grad_weight = lax.psum(local_weight, ("blk", "team"))
    return (layer_out, grad_features, grad_weight)


def solution(mesh):
    in_specs = (
        P(("blk", "team"), None),
        P(),
        P("blk", "team", None, None, None, None),
        P("blk", "team", None, None),
        P("blk", "team", None),
        P(("blk", "team"), None),
    )
    out_specs = (P(("blk", "team"), None), P(("blk", "team"), None), P())
    return jax.shard_map(body, mesh=mesh, in_specs=in_specs, out_specs=out_specs, check_vma=False)
```

profile of v0, /device:TPU:1, one launch (start us, length us, event | category | flops | bytes accessed | tf_op | source)
XLA Modules:
  0.0 1367.3 jit_solution(14644944449988133237)
XLA Ops:
  28.5 243.3 %while.32 = (s32[]{:T(128)}, bf16[128,256]{1,0:T(8,128)(2,1)S(1)}, f32[16,128,256]{2,1,0:T(8,128)S(1)}, s32[]{:T(128)}, s32[12,6]{0,1:T(8,128)S(1)}, /*index=5*/...) while((s32[]{:T(128)}, bf16[128,256]{1,0:T(8,128)(2,1)S(1)}, ...), condition=%wide.region_1.2_spmd, body=%wide.region_0.1_spmd.sunk | while | flops 50724880 | bytes 3801797 | solution.py:58
  28.5 3.9 collective-permute-start
  45.1 2.5 collective-permute-done
  52.8 1.9 collective-permute-start
  72.6 1.9 collective-permute-start
  92.4 10.2 collective-permute-start
  120.4 3.1 collective-permute-start
  141.4 3.1 collective-permute-start
  162.4 2.8 collective-permute-start
  183.1 8.1 collective-permute-start
  209.1 3.1 collective-permute-start
  230.1 3.1 collective-permute-start
  251.1 2.8 collective-permute-start
  273.2 282.9 %reduce-scatter.2.cloned.1.call-done = f32[32,256]{1,0:T(8,128)} async-done(((f32[2048,256]{1,0:T(8,128)}), f32[32,256]{1,0:T(8,128)}) %reduce-scatter.2.cloned.1.call-update) | async-done | bytes 32784 | tf_op jit(solution)/shard_map/reduce_scatter | solution.py:61
  557.7 3.0 copy.9
  561.5 116.5 %all-gather.2.cloned.1.call-done = bf16[2048,256]{1,0:T(8,128)(2,1)} async-done(((bf16[32,256]{1,0:T(8,128)(2,1)}), bf16[2048,256]{1,0:T(8,128)(2,1)}) %all-gather.2.cloned.1.call-update) | async-done | bytes 1048592 | tf_op jit(solution)/shard_map/all_gather | solution.py:67
  678.1 2.0 fusion.26
  681.9 202.4 %while.33 = (s32[]{:T(128)}, f32[128,256]{1,0:T(8,128)}, s32[]{:T(128)}, bf16[12,6,128,128]{2,3,1,0:T(8,128)(2,1)S(1)}, bf16[12,6,16]{2,1,0:T(8,128)(2,1)}, /*in...) while((s32[]{:T(128)}, f32[128,256]{1,0:T(8,128)}, s32[]{:T(128)}, ...), condition=%wide.region_4.5_spmd, body=%wide.region_3.4_spmd.sunk | while | flops 56655884 | bytes 2951413 | solution.py:73
  681.9 3.1 collective-permute-start.1
  686.4 8.7 collective-permute-done.1
  696.9 1.9 collective-permute-start.1
  700.2 8.7 collective-permute-done.1
  714.0 14.0 %collective-permute-done.1 = f32[128,256]{1,0:T(8,128)} collective-permute-done((f32[128,256]{1,0:T(8,128)}, f32[128,256]{1,0:T(8,128)}, u32[]{:S(2)}, u32[]{:S(2)}) %collective-permute-start.1) | collective-permute-done | bytes 131104 | tf_op jit(solution)/shard_map/while/body/eval_jaxpr/ppermute | solution.py:10
  733.1 9.5 collective-permute-done.1
  747.7 11.6 collective-permute-done.1
  764.5 16.5 %collective-permute-done.1 = f32[128,256]{1,0:T(8,128)} collective-permute-done((f32[128,256]{1,0:T(8,128)}, f32[128,256]{1,0:T(8,128)}, u32[]{:S(2)}, u32[]{:S(2)}) %collective-permute-start.1) | collective-permute-done | bytes 131104 | tf_op jit(solution)/shard_map/while/body/eval_jaxpr/ppermute | solution.py:10
  786.1 14.6 %collective-permute-done.1 = f32[128,256]{1,0:T(8,128)} collective-permute-done((f32[128,256]{1,0:T(8,128)}, f32[128,256]{1,0:T(8,128)}, u32[]{:S(2)}, u32[]{:S(2)}) %collective-permute-start.1) | collective-permute-done | bytes 131104 | tf_op jit(solution)/shard_map/while/body/eval_jaxpr/ppermute | solution.py:10
  805.8 13.6 collective-permute-done.1
  824.5 17.1 %collective-permute-done.1 = f32[128,256]{1,0:T(8,128)} collective-permute-done((f32[128,256]{1,0:T(8,128)}, f32[128,256]{1,0:T(8,128)}, u32[]{:S(2)}, u32[]{:S(2)}) %collective-permute-start.1) | collective-permute-done | bytes 131104 | tf_op jit(solution)/shard_map/while/body/eval_jaxpr/ppermute | solution.py:10
  846.7 13.6 collective-permute-done.1
  865.4 17.1 %collective-permute-done.1 = f32[128,256]{1,0:T(8,128)} collective-permute-done((f32[128,256]{1,0:T(8,128)}, f32[128,256]{1,0:T(8,128)}, u32[]{:S(2)}, u32[]{:S(2)}) %collective-permute-start.1) | collective-permute-done | bytes 131104 | tf_op jit(solution)/shard_map/while/body/eval_jaxpr/ppermute | solution.py:10
  887.9 471.1 %all-reduce.2.cloned.1.call-done = f32[256,256]{0,1:T(8,128)} async-done(((f32[256,256]{0,1:T(8,128)}), f32[256,256]{0,1:T(8,128)}) %all-reduce.2.cloned.1.call-update) | async-done | bytes 262160 | tf_op jit(solution)/shard_map/psum | solution.py:83
  (211 shorter events, 143.4 us)
Async XLA Ops:
  7.2 11.7 copy-start
  7.2 548.9 %reduce-scatter.2.cloned.1.call-start = ((), (), s32[]{:S(2)}) async-start(), calls=%async_computation.1 | async-start | bytes 2129920 | tf_op jit(solution)/shard_map/reduce_scatter | solution.py:61
  28.5 19.2 %collective-permute-start = (bf16[128,256]{1,0:T(8,128)(2,1)S(1)}, bf16[128,256]{1,0:T(8,128)(2,1)S(1)}, u32[]{:S(2)}, u32[]{:S(2)}) collective-permute-start(bf16[128,256]{1,0:T(8,128)(2,1)S(1)} %get-tuple-element.523), channel_id=1, source_target_pairs={{704,0},{0,64},{64,128},{128,192},{192,256},{256,320},{320,384},{3... | collective-permute-start | bytes 196616 | tf_op jit(solution)/shard_map/while/body/eval_jaxpr/ppermute | solution.py:10
  52.8 14.6 %collective-permute-start = (bf16[128,256]{1,0:T(8,128)(2,1)S(1)}, bf16[128,256]{1,0:T(8,128)(2,1)S(1)}, u32[]{:S(2)}, u32[]{:S(2)}) collective-permute-start(bf16[128,256]{1,0:T(8,128)(2,1)S(1)} %get-tuple-element.523), channel_id=1, source_target_pairs={{704,0},{0,64},{64,128},{128,192},{192,256},{256,320},{320,384},{3... | collective-permute-start | bytes 196616 | tf_op jit(solution)/shard_map/while/body/eval_jaxpr/ppermute | solution.py:10
  72.6 14.6 %collective-permute-start = (bf16[128,256]{1,0:T(8,128)(2,1)S(1)}, bf16[128,256]{1,0:T(8,128)(2,1)S(1)}, u32[]{:S(2)}, u32[]{:S(2)}) collective-permute-start(bf16[128,256]{1,0:T(8,128)(2,1)S(1)} %get-tuple-element.523), channel_id=1, source_target_pairs={{704,0},{0,64},{64,128},{128,192},{192,256},{256,320},{320,384},{3... | collective-permute-start | bytes 196616 | tf_op jit(solution)/shard_map/while/body/eval_jaxpr/ppermute | solution.py:10
  92.4 22.9 %collective-permute-start = (bf16[128,256]{1,0:T(8,128)(2,1)S(1)}, bf16[128,256]{1,0:T(8,128)(2,1)S(1)}, u32[]{:S(2)}, u32[]{:S(2)}) collective-permute-start(bf16[128,256]{1,0:T(8,128)(2,1)S(1)} %get-tuple-element.523), channel_id=1, source_target_pairs={{704,0},{0,64},{64,128},{128,192},{192,256},{256,320},{320,384},{3... | collective-permute-start | bytes 196616 | tf_op jit(solution)/shard_map/while/body/eval_jaxpr/ppermute | solution.py:10
  120.4 15.8 %collective-permute-start = (bf16[128,256]{1,0:T(8,128)(2,1)S(1)}, bf16[128,256]{1,0:T(8,128)(2,1)S(1)}, u32[]{:S(2)}, u32[]{:S(2)}) collective-permute-start(bf16[128,256]{1,0:T(8,128)(2,1)S(1)} %get-tuple-element.523), channel_id=1, source_target_pairs={{704,0},{0,64},{64,128},{128,192},{192,256},{256,320},{320,384},{3... | collective-permute-start | bytes 196616 | tf_op jit(solution)/shard_map/while/body/eval_jaxpr/ppermute | solution.py:10
  141.4 15.9 %collective-permute-start = (bf16[128,256]{1,0:T(8,128)(2,1)S(1)}, bf16[128,256]{1,0:T(8,128)(2,1)S(1)}, u32[]{:S(2)}, u32[]{:S(2)}) collective-permute-start(bf16[128,256]{1,0:T(8,128)(2,1)S(1)} %get-tuple-element.523), channel_id=1, source_target_pairs={{704,0},{0,64},{64,128},{128,192},{192,256},{256,320},{320,384},{3... | collective-permute-start | bytes 196616 | tf_op jit(solution)/shard_map/while/body/eval_jaxpr/ppermute | solution.py:10
  162.4 15.6 %collective-permute-start = (bf16[128,256]{1,0:T(8,128)(2,1)S(1)}, bf16[128,256]{1,0:T(8,128)(2,1)S(1)}, u32[]{:S(2)}, u32[]{:S(2)}) collective-permute-start(bf16[128,256]{1,0:T(8,128)(2,1)S(1)} %get-tuple-element.523), channel_id=1, source_target_pairs={{704,0},{0,64},{64,128},{128,192},{192,256},{256,320},{320,384},{3... | collective-permute-start | bytes 196616 | tf_op jit(solution)/shard_map/while/body/eval_jaxpr/ppermute | solution.py:10
  183.1 20.9 %collective-permute-start = (bf16[128,256]{1,0:T(8,128)(2,1)S(1)}, bf16[128,256]{1,0:T(8,128)(2,1)S(1)}, u32[]{:S(2)}, u32[]{:S(2)}) collective-permute-start(bf16[128,256]{1,0:T(8,128)(2,1)S(1)} %get-tuple-element.523), channel_id=1, source_target_pairs={{704,0},{0,64},{64,128},{128,192},{192,256},{256,320},{320,384},{3... | collective-permute-start | bytes 196616 | tf_op jit(solution)/shard_map/while/body/eval_jaxpr/ppermute | solution.py:10
  209.1 15.8 %collective-permute-start = (bf16[128,256]{1,0:T(8,128)(2,1)S(1)}, bf16[128,256]{1,0:T(8,128)(2,1)S(1)}, u32[]{:S(2)}, u32[]{:S(2)}) collective-permute-start(bf16[128,256]{1,0:T(8,128)(2,1)S(1)} %get-tuple-element.523), channel_id=1, source_target_pairs={{704,0},{0,64},{64,128},{128,192},{192,256},{256,320},{320,384},{3... | collective-permute-start | bytes 196616 | tf_op jit(solution)/shard_map/while/body/eval_jaxpr/ppermute | solution.py:10
  230.1 15.9 %collective-permute-start = (bf16[128,256]{1,0:T(8,128)(2,1)S(1)}, bf16[128,256]{1,0:T(8,128)(2,1)S(1)}, u32[]{:S(2)}, u32[]{:S(2)}) collective-permute-start(bf16[128,256]{1,0:T(8,128)(2,1)S(1)} %get-tuple-element.523), channel_id=1, source_target_pairs={{704,0},{0,64},{64,128},{128,192},{192,256},{256,320},{320,384},{3... | collective-permute-start | bytes 196616 | tf_op jit(solution)/shard_map/while/body/eval_jaxpr/ppermute | solution.py:10
  251.1 15.6 %collective-permute-start = (bf16[128,256]{1,0:T(8,128)(2,1)S(1)}, bf16[128,256]{1,0:T(8,128)(2,1)S(1)}, u32[]{:S(2)}, u32[]{:S(2)}) collective-permute-start(bf16[128,256]{1,0:T(8,128)(2,1)S(1)} %get-tuple-element.523), channel_id=1, source_target_pairs={{704,0},{0,64},{64,128},{128,192},{192,256},{256,320},{320,384},{3... | collective-permute-start | bytes 196616 | tf_op jit(solution)/shard_map/while/body/eval_jaxpr/ppermute | solution.py:10
  271.8 1.3 copy-start.2
  271.8 284.3 %copy-start.4 = (bf16[32,256]{1,0:T(8,128)(2,1)S(1)}, bf16[32,256]{1,0:T(8,128)(2,1)}, u32[]{:S(2)}) copy-start(bf16[32,256]{1,0:T(8,128)(2,1)} %param.15) | copy-start | bytes 49156
  271.8 285.8 %copy-start.3 = (s32[1,1,12,6]{2,1,3,0:T(1,128)S(1)}, s32[1,1,12,6]{2,1,3,0:T(1,128)}, u32[]{:S(2)}) copy-start(s32[1,1,12,6]{2,1,3,0:T(1,128)} %param.13) | copy-start | bytes 868
  273.2 404.9 %all-gather.2.cloned.1.call-start = ((), (), s32[]{:S(2)}) async-start(), calls=%async_computation.2 | async-start | bytes 1064960 | tf_op jit(solution)/shard_map/all_gather | solution.py:67
  557.5 801.4 %all-reduce.2.cloned.1.call-start = ((), (), s32[]{:S(2)}) async-start(), calls=%async_computation.3 | async-start | bytes 524288 | tf_op jit(solution)/shard_map/psum | solution.py:83
  678.1 3.8 copy-start.1
  681.9 13.2 collective-permute-start.1
  696.9 12.0 collective-permute-start.1
  710.7 17.3 %collective-permute-start.1 = (f32[128,256]{1,0:T(8,128)}, f32[128,256]{1,0:T(8,128)}, u32[]{:S(2)}, u32[]{:S(2)}) collective-permute-start(f32[128,256]{1,0:T(8,128)} %get-tuple-element.554), channel_id=1, source_target_pairs={{704,0},{0,64},{64,128},{128,192},{192,256},{256,320},{320,384},{3... | collective-permute-start | bytes 393224 | tf_op jit(solution)/shard_map/while/body/eval_jaxpr/ppermute | solution.py:10
  729.8 12.8 collective-permute-start.1
  744.5 14.9 %collective-permute-start.1 = (f32[128,256]{1,0:T(8,128)}, f32[128,256]{1,0:T(8,128)}, u32[]{:S(2)}, u32[]{:S(2)}) collective-permute-start(f32[128,256]{1,0:T(8,128)} %get-tuple-element.554), channel_id=1, source_target_pairs={{704,0},{0,64},{64,128},{128,192},{192,256},{256,320},{320,384},{3... | collective-permute-start | bytes 393224 | tf_op jit(solution)/shard_map/while/body/eval_jaxpr/ppermute | solution.py:10
  761.2 19.8 %collective-permute-start.1 = (f32[128,256]{1,0:T(8,128)}, f32[128,256]{1,0:T(8,128)}, u32[]{:S(2)}, u32[]{:S(2)}) collective-permute-start(f32[128,256]{1,0:T(8,128)} %get-tuple-element.554), channel_id=1, source_target_pairs={{704,0},{0,64},{64,128},{128,192},{192,256},{256,320},{320,384},{3... | collective-permute-start | bytes 393224 | tf_op jit(solution)/shard_map/while/body/eval_jaxpr/ppermute | solution.py:10
  782.8 17.9 %collective-permute-start.1 = (f32[128,256]{1,0:T(8,128)}, f32[128,256]{1,0:T(8,128)}, u32[]{:S(2)}, u32[]{:S(2)}) collective-permute-start(f32[128,256]{1,0:T(8,128)} %get-tuple-element.554), channel_id=1, source_target_pairs={{704,0},{0,64},{64,128},{128,192},{192,256},{256,320},{320,384},{3... | collective-permute-start | bytes 393224 | tf_op jit(solution)/shard_map/while/body/eval_jaxpr/ppermute | solution.py:10
  802.5 16.9 %collective-permute-start.1 = (f32[128,256]{1,0:T(8,128)}, f32[128,256]{1,0:T(8,128)}, u32[]{:S(2)}, u32[]{:S(2)}) collective-permute-start(f32[128,256]{1,0:T(8,128)} %get-tuple-element.554), channel_id=1, source_target_pairs={{704,0},{0,64},{64,128},{128,192},{192,256},{256,320},{320,384},{3... | collective-permute-start | bytes 393224 | tf_op jit(solution)/shard_map/while/body/eval_jaxpr/ppermute | solution.py:10
  821.2 20.4 %collective-permute-start.1 = (f32[128,256]{1,0:T(8,128)}, f32[128,256]{1,0:T(8,128)}, u32[]{:S(2)}, u32[]{:S(2)}) collective-permute-start(f32[128,256]{1,0:T(8,128)} %get-tuple-element.554), channel_id=1, source_target_pairs={{704,0},{0,64},{64,128},{128,192},{192,256},{256,320},{320,384},{3... | collective-permute-start | bytes 393224 | tf_op jit(solution)/shard_map/while/body/eval_jaxpr/ppermute | solution.py:10
  843.4 16.9 %collective-permute-start.1 = (f32[128,256]{1,0:T(8,128)}, f32[128,256]{1,0:T(8,128)}, u32[]{:S(2)}, u32[]{:S(2)}) collective-permute-start(f32[128,256]{1,0:T(8,128)} %get-tuple-element.554), channel_id=1, source_target_pairs={{704,0},{0,64},{64,128},{128,192},{192,256},{256,320},{320,384},{3... | collective-permute-start | bytes 393224 | tf_op jit(solution)/shard_map/while/body/eval_jaxpr/ppermute | solution.py:10
  862.1 20.4 %collective-permute-start.1 = (f32[128,256]{1,0:T(8,128)}, f32[128,256]{1,0:T(8,128)}, u32[]{:S(2)}, u32[]{:S(2)}) collective-permute-start(f32[128,256]{1,0:T(8,128)} %get-tuple-element.554), channel_id=1, source_target_pairs={{704,0},{0,64},{64,128},{128,192},{192,256},{256,320},{320,384},{3... | collective-permute-start | bytes 393224 | tf_op jit(solution)/shard_map/while/body/eval_jaxpr/ppermute | solution.py:10
Sparse Core Ops, SparseCore 0:
  273.3 282.7 reduce-scatter.1
  559.4 118.6 all-gather.1
  886.3 472.6 all-reduce.1
where the time goes:
time: 1370 us
  waiting for transfers between devices  1020 us (74%)
  loops' own time  126 us (9%)
  starting transfers between devices  66.5 us (5%)
  matrix products  56.9 us (4%)
  other arithmetic  49.8 us (4%)
  between operations  25.3 us (2%)
  local copies, waits for them, and re-layouts  24.3 us (2%)
    psum x1, waiting for transfers between devices, body(): grad_weight = lax.psum(local_weight, ('blk', 'team'))  471 us
    reduce_scatter x1, waiting for transfers between devices, body(): lax.psum_scatter(partial_value.reshape(block_rows, width), 'team', scatte...  283 us
    ppermute x22, waiting for transfers between devices, from_behind(): return lax.ppermute(block, axis, route)  148 us
    another operation x1, loops' own time, body(): lax.fori_loop(1, blocks, forward_step, (hidden, forward_term(empty_full,...  126 us
    all_gather x1, waiting for transfers between devices, body(): lax.all_gather(grad_pre, 'team', axis=0, tiled=True)  117 us
    ppermute x22, starting transfers between devices, from_behind(): return lax.ppermute(block, axis, route)  66.4 us
    dynamic_update_slice x72, other arithmetic, forward_term(): lax.dynamic_update_index_in_dim(acc, current + live_c[slot] * prod[slot],...  47 us
  transfers between devices with their start and end apart: 25, of which 15 were waited for; matrix products, arithmetic and copies ran while one was open for 3% of the time, Pallas kernels for 0%

commit v1 on v0

v1 whole, which is shorter than its diff:
```python
import functools

import jax
import jax.numpy as jnp
from jax import lax
from jax.experimental import pallas as pl
from jax.experimental.pallas import tpu as pltpu
from jax.sharding import PartitionSpec as P

MESH = pl.DeviceIdType.MESH
BF = jnp.bfloat16
F32 = jnp.float32
ZH, NX, ZL, NY = 3, 4, 4, 8
NC = ZH * NX
SLOTS, RT, TILE, HALF, OWN = 6, 16, 128, 128, 32
NTILES = NC * SLOTS
N_COPIES = 160


def kernel(
    feat, weight, tiles, rows, counts, gout,
    out, gfeat, gweight,
    tb, tT, inv, ridx, xs, acc, pc, rc, s, ry0, rz0, rz1, ry1, t0, t1, gg0, gg1,
    part, fa, fb, fc, ff, fs, fz, gw1s, gw1, gw2s, gw2, gw3, gw4, gw5, gwa,
    tile_sem, send_sem, recv_sem,
):
    blk, team = lax.axis_index("blk"), lax.axis_index("team")
    zh, x = blk // NX, blk % NX
    zl, y, co = team // (2 * NY), (team // 2) % NY, team % 2

    def at(zh_=zh, x_=x, zl_=zl, y_=y, co_=co):
        return (zh_ * NX + x_, (zl_ * NY + y_) * 2 + co_)

    def off(value, d, size):
        return (value + d + size) % size

    started = []

    def send(src, dst, device):
        i = len(started)
        copy = pltpu.make_async_remote_copy(
            src_ref=src, dst_ref=dst, send_sem=send_sem.at[i], recv_sem=recv_sem.at[i],
            device_id=device, device_id_type=MESH,
        )
        copy.start()
        started.append(copy)
        return copy

    barrier = pltpu.get_barrier_semaphore()
    partners = [at(co_=1 - co)]
    partners += [at(y_=off(y, d, NY)) for d in range(1, NY)]
    partners += [at(zl_=off(zl, d, ZL)) for d in range(1, ZL)]
    partners += [at(x_=off(x, d, NX)) for d in range(1, NX)]
    partners += [at(zh_=off(zh, d, ZH)) for d in range(1, ZH)]
    for device in partners:
        pl.semaphore_signal(barrier, inc=1, device_id=device, device_id_type=MESH)
    load = pltpu.make_async_copy(tiles, tb.at[pl.ds(0, NTILES)], tile_sem)
    load.start()
    for h in range(2):
        xs[h, blk] = feat[:, h * HALF:(h + 1) * HALF]
    tb[NTILES] = jnp.zeros((TILE, TILE), BF)
    for ref in (gg0, gg1):
        ref[ZL] = jnp.zeros((NY, 2, OWN, HALF), BF)

    def index_body(c, carry):
        count = counts[0, 0, c]
        rowof = [jnp.where(k < count, rows[0, 0, c, k], RT) for k in range(SLOTS)]
        for k in range(SLOTS):
            ridx[c * SLOTS + k] = rowof[k]
        for r in range(RT):
            found = NTILES
            for k in range(SLOTS):
                found = jnp.where(rowof[k] == r, c * SLOTS + k, found)
            inv[c * RT + r] = found
        return carry

    lax.fori_loop(0, NC, index_body, 0)
    pl.semaphore_wait(barrier, len(partners))

    own_z, own_x = [], []
    sign = (1, -1)
    for h in range(2):
        block = xs.at[h, blk]
        own_z.append([send(block, block, at(zh_=off(zh, d, ZH))) for d in range(1, ZH)])
        own_x.append([send(block, block, at(x_=off(x, sign[h], NX))), send(block, block, at(x_=off(x, -sign[h], NX)))])

    def slot(dz, dx):
        return off(zh, dz, ZH) * NX + off(x, dx, NX)

    def forward_group(h, dz, first):
        cols = [slot(dz, dx) for dx in range(NX)]
        right = jnp.concatenate([xs[h, c] for c in cols], axis=0)

        def step(r, carry):
            left = jnp.concatenate([tb[inv[c * RT + r]] for c in cols], axis=1)
            prod = jnp.dot(left, right, preferred_element_type=F32).reshape(2, 2, OWN, HALF)
            zt, yt = r // (NY // 2), (r % (NY // 2)) * 2
            if first:
                acc[h, zt, pl.ds(yt, 2)] = prod
            else:
                acc[h, zt, pl.ds(yt, 2)] += prod
            return carry

        lax.fori_loop(0, RT, step, 0, unroll=2)

    def pass_on(h, dz):
        block = xs.at[h, slot(dz, -sign[h])]
        return send(block, block, at(x_=off(x, sign[h], NX)))

    far = [[None] * ZH, [None] * ZH]
    near = [[None] * ZH, [None] * ZH]
    load.wait()
    for h in range(2):
        own_x[h][0].wait_recv()
        far[h][0] = pass_on(h, 0)

    def spread(h):
        for d in range(1, ZH):
            own_z[h][d - 1].wait_recv()
            block = xs.at[h, slot(-d, 0)]
            near[h][ZH - d] = [
                send(block, block, at(x_=off(x, sign[h], NX))),
                send(block, block, at(x_=off(x, -sign[h], NX))),
            ]

    def group_zero(h):
        own_x[h][1].wait_recv()
        far[h][0].wait_recv()
        forward_group(h, 0, True)

    def relay(h):
        for d in range(1, ZH):
            near[h][ZH - d][0].wait_recv()
            far[h][ZH - d] = pass_on(h, ZH - d)

    def group_rest(h):
        for d in range(1, ZH):
            near[h][ZH - d][1].wait_recv()
            far[h][ZH - d].wait_recv()
            forward_group(h, ZH - d, False)

    def to_partner_core(h):
        pc[h] = acc[h, :, :, 1 - co].astype(BF)
        return send(pc.at[h], rc.at[h], at(co_=1 - co))

    def add_partner_core(h, copy):
        copy.wait_recv()
        s[h] = (acc[h, :, :, co] + rc[h].astype(F32)).astype(BF)

    def transpose_body(c, carry):
        for k in range(SLOTS):
            tT[c, :, k * TILE:(k + 1) * TILE] = tb[c * SLOTS + k].T
        return carry

    spread(0)
    group_zero(0)
    relay(0)
    spread(1)
    group_rest(0)
    core0 = to_partner_core(0)
    relay(1)
    group_zero(1)
    add_partner_core(0, core0)
    y0 = [send(s.at[0, :, off(y, d, NY)], ry0.at[d], at(y_=off(y, d, NY))) for d in range(1, NY)]
    group_rest(1)
    core1 = to_partner_core(1)
    lax.fori_loop(0, NC // 2, transpose_body, 0)
    add_partner_core(1, core1)
    z1 = [send(s.at[1, off(zl, d, ZL)], rz1.at[d], at(zl_=off(zl, d, ZL))) for d in range(1, ZL)]
    lax.fori_loop(NC // 2, NC, transpose_body, 0)

    total = s[0, :, y].astype(F32)
    for d in range(1, NY):
        y0[d - 1].wait_recv()
        total += ry0[d].astype(F32)
    t0[...] = total.astype(BF)
    z0 = [send(t0.at[off(zl, d, ZL)], rz0.at[d], at(zl_=off(zl, d, ZL))) for d in range(1, ZL)]
    total = s[1, zl].astype(F32)
    for d in range(1, ZL):
        z1[d - 1].wait_recv()
        total += rz1[d].astype(F32)
    t1[...] = total.astype(BF)
    y1 = [send(t1.at[off(y, d, NY)], ry1.at[d], at(y_=off(y, d, NY))) for d in range(1, NY)]
    ax0 = t0[zl].astype(F32)
    for d in range(1, ZL):
        z0[d - 1].wait_recv()
        ax0 += rz0[d].astype(F32)
    ax1 = t1[y].astype(F32)
    for d in range(1, NY):
        y1[d - 1].wait_recv()
        ax1 += ry1[d].astype(F32)

    ax = jnp.concatenate([ax0, ax1], axis=1)
    high = ax.astype(BF)
    low = (ax - high.astype(F32)).astype(BF)
    w = weight[...]
    pre = jnp.dot(high, w, preferred_element_type=F32) + jnp.dot(low, w, preferred_element_type=F32)
    sig = jax.nn.sigmoid(pre)
    out[...] = (pre * sig).astype(BF)
    grad = (gout[...].astype(F32) * sig * (1.0 + pre * (1.0 - sig))).astype(BF)
    back = lax.dot_general(grad, w, (((1,), (1,)), ((), ())), preferred_element_type=F32).astype(BF)
    gg0[zl, y, co] = back[:, :HALF]
    gg1[zl, y, co] = back[:, HALF:]

    mine0, mine1 = gg0.at[zl, y, co], gg1.at[zl, y, co]
    a0 = [send(mine0, mine0, at(zl_=off(zl, d, ZL))) for d in range(1, ZL)]
    a1 = [send(mine1, mine1, at(y_=off(y, d, NY))) for d in range(1, NY)]

    gw = lax.dot_general(
        jnp.concatenate([high, low], axis=0), jnp.concatenate([grad, grad], axis=0),
        (((0,), (0,)), ((), ())), preferred_element_type=F32,
    ).reshape(2, TILE, 2 * HALF)
    gw1s[...] = gw
    g1 = send(gw1s.at[1 - co], gw1, at(co_=1 - co))

    other = at(co_=1 - co)
    for copy in a0:
        copy.wait_recv()
    line = gg0.at[pl.ds(0, ZL), y, co]
    b0 = [send(line, line, at(y_=off(y, d, NY))) for d in range(1, NY)]
    c0 = [send(line, line, other)]
    for copy in a1:
        copy.wait_recv()
    line = gg1.at[zl, :, co]
    b1 = [send(line, line, at(zl_=off(zl, d, ZL))) for d in range(1, ZL)]
    c1 = [send(line, line, other)]
    g1.wait_recv()
    gw2s[...] = (gw1s[co] + gw1[...]).reshape(NY, OWN // 2, 2 * HALF).astype(BF)
    g2 = [send(gw2s.at[off(y, d, NY)], gw2.at[d], at(y_=off(y, d, NY))) for d in range(1, NY)]
    for d in range(1, NY):
        b0[d - 1].wait_recv()
        line = gg0.at[pl.ds(0, ZL), off(y, -d, NY), co]
        c0.append(send(line, line, other))
    for d in range(1, ZL):
        b1[d - 1].wait_recv()
        line = gg1.at[off(zl, -d, ZL), :, co]
        c1.append(send(line, line, other))
    sub = gw2s[y].astype(F32)
    for d in range(1, NY):
        g2[d - 1].wait_recv()
        sub += gw2[d].astype(F32)
    gw3[x] = sub
    g3 = [send(gw3.at[x], gw3.at[x], at(x_=off(x, d, NX))) for d in range(1, NX)]

    def back_term(h, dz, dx):
        ref = (gg0, gg1)[h]
        c = slot(dz, dx)
        picks = []
        for k in range(SLOTS):
            r = ridx[c * SLOTS + k]
            picks.append(ref[r >> 2, pl.ds((r & 3) * 2, 2)].reshape(TILE, HALF))
        return jnp.dot(tT[c], jnp.concatenate(picks, axis=0), preferred_element_type=F32)

    order = (1, 2, 0)

    def first_products(h):
        ahead, behind = at(x_=off(x, sign[h], NX)), at(x_=off(x, -sign[h], NX))
        sa, sb = {}, {}
        for dz in order:
            part[h, 0, dz] = back_term(h, dz, 2).astype(BF)
            sa[dz] = send(part.at[h, 0, dz], fa.at[h, dz], ahead)
            part[h, 1, dz] = back_term(h, dz, -sign[h]).astype(BF)
            sb[dz] = send(part.at[h, 1, dz], fb.at[h, dz], behind)
        return sa, sb

    def second_products(h, sa):
        ahead = at(x_=off(x, sign[h], NX))
        sc = {}
        for dz in order:
            term = back_term(h, dz, sign[h])
            sa[dz].wait_recv()
            ff[h, dz] = (term + fa[h, dz].astype(F32)).astype(BF)
            sc[dz] = send(ff.at[h, dz], fc.at[h, dz], ahead)
        return sc

    def last_products(h, sb, sc):
        sz = []
        for dz in order:
            term = back_term(h, dz, 0)
            sb[dz].wait_recv()
            term += fb[h, dz].astype(F32)
            sc[dz].wait_recv()
            term += fc[h, dz].astype(F32)
            if dz:
                fs[h, dz - 1] = term.astype(BF)
                sz.append(send(fs.at[h, dz - 1], fz.at[h, dz - 1], at(zh_=off(zh, dz, ZH))))
        return sz, term

    def finish(h, sz, term):
        for dz in range(1, ZH):
            sz[dz - 1].wait_recv()
            term += fz[h, dz - 1].astype(F32)
        gfeat[:, h * HALF:(h + 1) * HALF] = term.astype(BF)

    for copy in c0:
        copy.wait_recv()
    sa0, sb0 = first_products(0)
    for copy in c1:
        copy.wait_recv()
    sa1, sb1 = first_products(1)
    sc0 = second_products(0, sa0)
    for copy in g3:
        copy.wait_recv()
    gw4[zl] = (gw3[0] + gw3[1]) + (gw3[2] + gw3[3])
    g4 = [send(gw4.at[zl], gw4.at[zl], at(zl_=off(zl, d, ZL))) for d in range(1, ZL)]
    sc1 = second_products(1, sa1)
    sz0, term0 = last_products(0, sb0, sc0)
    for copy in g4:
        copy.wait_recv()
    gw5[zh] = (gw4[0] + gw4[1]) + (gw4[2] + gw4[3])
    g5 = [send(gw5.at[zh], gw5.at[zh], at(zh_=off(zh, d, ZH))) for d in range(1, ZH)]
    sz1, term1 = last_products(1, sb1, sc1)
    for copy in g5:
        copy.wait_recv()
    gwa[co, y] = gw5[0] + gw5[1] + gw5[2]
    g6 = [send(gwa.at[co, y], gwa.at[co, y], at(y_=off(y, d, NY))) for d in range(1, NY)]
    finish(0, sz0, term0)
    for copy in g6:
        copy.wait_recv()
    g7 = send(gwa.at[co], gwa.at[co], other)
    finish(1, sz1, term1)
    g7.wait_recv()
    gweight[...] = gwa[...].reshape(2 * HALF, 2 * HALF)
    for copy in started:
        copy.wait_send()


def body(features, weight, tile_values, tile_rows, tile_counts, grad_out):
    vmem = pl.BlockSpec(memory_space=pltpu.VMEM)
    smem = pl.BlockSpec(memory_space=pltpu.SMEM)
    rows16 = OWN // 2
    return pl.pallas_call(
        kernel,
        out_shape=(
            jax.ShapeDtypeStruct(grad_out.shape, BF),
            jax.ShapeDtypeStruct(features.shape, BF),
            jax.ShapeDtypeStruct(weight.shape, F32),
        ),
        in_specs=[vmem, vmem, pl.BlockSpec(memory_space=pl.ANY), smem, smem, vmem],
        out_specs=(vmem, vmem, vmem),
        scratch_shapes=[
            pltpu.VMEM((NTILES + 1, TILE, TILE), BF),
            pltpu.VMEM((NC, TILE, SLOTS * TILE), BF),
            pltpu.SMEM((NC * RT,), jnp.int32),
            pltpu.SMEM((NTILES,), jnp.int32),
            pltpu.VMEM((2, NC, TILE, HALF), BF),
            pltpu.VMEM((2, ZL, NY, 2, OWN, HALF), F32),
            pltpu.VMEM((2, ZL, NY, OWN, HALF), BF),
            pltpu.VMEM((2, ZL, NY, OWN, HALF), BF),
            pltpu.VMEM((2, ZL, NY, OWN, HALF), BF),
            pltpu.VMEM((NY, ZL, OWN, HALF), BF),
            pltpu.VMEM((ZL, OWN, HALF), BF),
            pltpu.VMEM((ZL, NY, OWN, HALF), BF),
            pltpu.VMEM((NY, OWN, HALF), BF),
            pltpu.VMEM((ZL, OWN, HALF), BF),
            pltpu.VMEM((NY, OWN, HALF), BF),
            pltpu.VMEM((ZL + 1, NY, 2, OWN, HALF), BF),
            pltpu.VMEM((ZL + 1, NY, 2, OWN, HALF), BF),
            pltpu.VMEM((2, 2, ZH, TILE, HALF), BF),
            pltpu.VMEM((2, ZH, TILE, HALF), BF),
            pltpu.VMEM((2, ZH, TILE, HALF), BF),
            pltpu.VMEM((2, ZH, TILE, HALF), BF),
            pltpu.VMEM((2, ZH, TILE, HALF), BF),
            pltpu.VMEM((2, ZH - 1, TILE, HALF), BF),
            pltpu.VMEM((2, ZH - 1, TILE, HALF), BF),
            pltpu.VMEM((2, TILE, 2 * HALF), F32),
            pltpu.VMEM((TILE, 2 * HALF), F32),
            pltpu.VMEM((NY, rows16, 2 * HALF), BF),
            pltpu.VMEM((NY, rows16, 2 * HALF), BF),
            pltpu.VMEM((NX, rows16, 2 * HALF), F32),
            pltpu.VMEM((ZL, rows16, 2 * HALF), F32),
            pltpu.VMEM((ZH, rows16, 2 * HALF), F32),
            pltpu.VMEM((2, NY, rows16, 2 * HALF), F32),
            pltpu.SemaphoreType.DMA,
            pltpu.SemaphoreType.DMA((N_COPIES,)),
            pltpu.SemaphoreType.DMA((N_COPIES,)),
        ],
        compiler_params=pltpu.CompilerParams(
            collective_id=0, has_side_effects=True, vmem_limit_bytes=40 * 2 ** 20
        ),
    )(features, weight, tile_values.reshape(NTILES, TILE, TILE), tile_rows, tile_counts, grad_out)


def solution(mesh):
    in_specs = (
        P(("blk", "team"), None),
        P(),
        P("blk", "team", None, None, None, None),
        P("blk", "team", None, None),
        P("blk", "team", None),
        P(("blk", "team"), None),
    )
    out_specs = (P(("blk", "team"), None), P(("blk", "team"), None), P())
    return jax.shard_map(body, mesh=mesh, in_specs=in_specs, out_specs=out_specs, check_vma=False)
```

time: 1370 us -> 110 us (0.08)
  waiting for transfers between devices: 1020 us -> 0 us
  loops' own time: 126 us -> 0 us
  Pallas kernels: 0 us -> 101 us
  starting transfers between devices: 66.5 us -> 0 us
  matrix products: 56.9 us -> 0 us
  other arithmetic: 49.8 us -> 0 us
  between operations: 25.3 us -> 0.64 us
  local copies, waits for them, and re-layouts: 24.3 us -> 7.49 us
    psum x1 -> x0, waiting for transfers between devices: 471 us -> none  [body(): grad_weight = lax.psum(local_weight, ('blk', 'team'))]
    reduce_scatter x1 -> x0, waiting for transfers between devices: 283 us -> none  [body(): lax.psum_scatter(partial_value.reshape(block_rows, width), 'team', scatte...]
    ppermute x22 -> x0, waiting for transfers between devices: 148 us -> none  [from_behind(): return lax.ppermute(block, axis, route)]
    another operation x2 -> x0, loops' own time: 126 us -> none  [the longest x1 126 us: body(): lax.fori_loop(1, blocks, forward_step, (hidden, forward_term(empty_full,...]
    all_gather x1 -> x0, waiting for transfers between devices: 117 us -> none  [body(): lax.all_gather(grad_pre, 'team', axis=0, tiled=True)]
    pallas_call x0 -> x1, Pallas kernels: none -> 101 us  [body(): pl.pallas_call(kernel, out_shape=(jax.ShapeDtypeStruct(grad_out.shape, BF...]
    ppermute x22 -> x0, starting transfers between devices: 66.4 us -> none  [from_behind(): return lax.ppermute(block, axis, route)]
    dot_general x39 -> x0, matrix products: 56.9 us -> none  [the longest x12 21.7 us: backward_term(): jnp.einsum('kij,kif->jf', tiles_c, chosen, preferred_element_type=jnp.flo...]
  transfers between devices with their start and end apart: 25 -> 0, of which waited for: 15 -> 0; matrix products, arithmetic and copies ran while one was open for 3% -> 0% of each run, Pallas kernels for 0% -> 0%
where the time goes in v1:
time: 110 us
  Pallas kernels  101 us (92%)
  local copies, waits for them, and re-layouts  7.49 us (7%)
    pallas_call x1, Pallas kernels, body(): pl.pallas_call(kernel, out_shape=(jax.ShapeDtypeStruct(grad_out.shape, BF...  101 us
    unnamed x14, local copies, waits for them, and re-layouts  7.49 us

profile of v1, /device:TPU:1, one launch (start us, length us, event | category | flops | bytes accessed | tf_op | source)
XLA Modules:
  0.0 109.5 jit_solution(12493014793476733582)
XLA Ops:
  0.6 0.8 copy.9.rows
  1.4 0.0 copy-start
  1.4 1.7 %copy-done = bf16[1,1,12,6,128,128]{5,4,3,2,1,0:T(8,128)(2,1)S(1)} copy-done((bf16[1,1,12,6,128,128]{5,4,3,2,1,0:T(8,128)(2,1)S(1)}, bf16[1,1,12,6,128,128]{5,4,3,2,1,0:T(8,128)(2,1)}, u32[]{:S(2)}) %copy-start) | copy-done | bytes 2359320
  3.1 0.0 copy-start.1
  3.1 0.9 copy-done.1
  4.0 0.0 copy-start.2
  4.0 0.8 copy-done.2
  4.8 0.0 copy-start.3
  4.8 0.7 copy-done.3
  5.5 0.0 copy-start.4
  5.5 0.7 copy-done.4
  6.2 101.4 %shard_map.85 = (bf16[32,256]{1,0:T(8,128)(2,1)S(1)}, bf16[128,256]{1,0:T(8,128)(2,1)S(1)}, f32[256,256]{1,0:T(8,128)S(1)}) custom-call(bf16[128,256]{1,0:T(8,128)(2,1)S(1)} %copy-done.2, bf16[256,256]{1,0:T(8,128)(2,1)S(1)} %copy-done.1, bf16[72,128,128]{2,1,0:T(8,128)(2,1)S(1)} %bitcast.1, s32[1,1,12,6]{3,2,1,0:T(8,128)S(1)} %copy.9.rows, ...), custom_call_target="tpu_custom_call" | custom-call | tf_op jit(solution)/shard_map/pallas_call | solution.py:332
  107.6 0.6 copy.13
  108.2 0.6 copy.14
  108.8 0.7 copy.15
Async XLA Ops:
  1.4 1.7 %copy-start = (bf16[1,1,12,6,128,128]{5,4,3,2,1,0:T(8,128)(2,1)S(1)}, bf16[1,1,12,6,128,128]{5,4,3,2,1,0:T(8,128)(2,1)}, u32[]{:S(2)}) copy-start(bf16[1,1,12,6,128,128]{5,4,3,2,1,0:T(8,128)(2,1)} %param.8) | copy-start | bytes 7077892
  3.1 0.9 copy-start.1
  4.0 0.8 copy-start.2
  4.8 0.7 copy-start.3
  5.5 0.7 copy-start.4

commit v2 on v0

v2 whole, which is shorter than its diff:
```python
import math

import jax
import jax.numpy as jnp
from jax import lax
from jax.experimental import pallas as pl
from jax.experimental.pallas import tpu as pltpu
from jax.sharding import PartitionSpec as P

MESH = pl.DeviceIdType.MESH
BF = jnp.bfloat16
F32 = jnp.float32
ZH, NX, ZL, NY = 3, 4, 4, 8
NC = ZH * NX
SLOTS, RT, TILE, HALF, OWN = 6, 16, 128, 128, 32
NTILES = NC * SLOTS
N_GROUPS, N_UNITS = 47, 320


def kernel(
    feat, weight, tiles, rows_in, counts_in, gout_in,
    out, gfeat, gweight,
    tb, tT, wv, gout, rows, counts, inv_v, ridx_v, inv, ridx, xs, acc, pc, rc, s, ry0, rz0, rz1, ry1, t0, t1, gg0, gg1,
    part, fx, own, fs, fz, gw1s, gw1, gw2s, gw2, gw3, gw4, gw5, gwa,
    spare, load_sem, send_sem, recv_sem,
):
    blk, team = lax.axis_index("blk"), lax.axis_index("team")
    zh, x = blk // NX, blk % NX
    zl, y, co = team // (2 * NY), (team // 2) % NY, team % 2

    def at(zh_=zh, x_=x, zl_=zl, y_=y, co_=co):
        return (zh_ * NX + x_, (zl_ * NY + y_) * 2 + co_)

    def off(value, d, size):
        return (value + d + size) % size

    other = at(co_=1 - co)
    x_peers = [at(x_=off(x, d, NX)) for d in range(1, NX)]
    y_peers = [at(y_=off(y, d, NY)) for d in range(1, NY)]
    zl_peers = [at(zl_=off(zl, d, ZL)) for d in range(1, ZL)]
    zh_peers = [at(zh_=off(zh, d, ZH)) for d in range(1, ZH)]

    barrier = pltpu.get_barrier_semaphore()
    partners = zh_peers + y_peers + x_peers + zl_peers + [other]
    for device in partners:
        pl.semaphore_signal(barrier, inc=1, device_id=device, device_id_type=MESH)

    loads = []

    def load(src, dst):
        copy = pltpu.make_async_copy(src, dst, load_sem.at[len(loads)])
        copy.start()
        loads.append(copy)
        return copy

    load_x = [load(feat.at[:, h * HALF:(h + 1) * HALF], xs.at[h, blk]) for h in range(2)]
    load_index = [load(rows_in, rows), load(counts_in, counts)]
    load_tiles = load(tiles, tb.at[pl.ds(0, NTILES)])
    load_rest = [load(weight, wv), load(gout_in, gout)]

    unit = OWN * HALF * 2
    groups, sent = [], [0, 0]

    def remote(src, dst, group, phase, device):
        return pltpu.make_async_remote_copy(
            src_ref=src, dst_ref=dst, send_sem=send_sem.at[phase], recv_sem=recv_sem.at[group],
            device_id=device, device_id_type=MESH,
        )

    def size(ref):
        return math.prod(ref.shape) * ref.dtype.itemsize // unit

    class Group:
        def __init__(self, phase):
            self.index, self.phase, self.units = len(groups), phase, 0
            groups.append(self)

        def count(self, units):
            self.units += units
            sent[self.phase] += units

        def send(self, src, dst, device):
            remote(src, dst, self.index, self.phase, device).start()
            self.count(size(src))

        def wait(self):
            ref = spare.at[pl.ds(0, self.units)]
            remote(ref, ref, self.index, self.phase, other).wait_recv()

    def send_all(phase, sources, targets, devices):
        group = Group(phase)
        for src, dst, device in zip(sources, targets, devices):
            group.send(src, dst, device)
        return group

    def send_same(phase, ref, devices):
        return send_all(phase, [ref] * len(devices), [ref] * len(devices), devices)

    for copy in load_x:
        copy.wait()
    pl.semaphore_wait(barrier, len(partners))

    own_z = [[send_same(0, xs.at[h, blk], [device]) for device in zh_peers] for h in range(2)]
    own_x = [send_same(0, xs.at[h, blk], x_peers) for h in range(2)]

    tb[NTILES] = jnp.zeros((TILE, TILE), BF)
    for ref in (gg0, gg1):
        ref[ZL] = jnp.zeros((NY, 2, OWN, HALF), BF)

    for copy in load_index:
        copy.wait()
    live = counts[...]
    first_tile = lax.broadcasted_iota(jnp.int32, (1, NC), 1) * SLOTS
    rowof = [jnp.where(k < live, rows[k], RT) for k in range(SLOTS)]
    for k in range(SLOTS):
        ridx_v[k] = rowof[k]
    for r in range(RT):
        found = jnp.full((1, NC), NTILES, jnp.int32)
        for k in range(SLOTS):
            found = jnp.where(rowof[k] == r, first_tile + k, found)
        inv_v[r] = found
    load_index = [load(inv_v, inv), load(ridx_v, ridx)]
    for copy in load_index:
        copy.wait()
    load_tiles.wait()

    def slot(dz, dx):
        return off(zh, dz, ZH) * NX + off(x, dx, NX)

    def forward_group(h, dz, first, last):
        cols = [slot(dz, dx) for dx in range(NX)]
        right = jnp.concatenate([xs[h, c] for c in cols], axis=0)

        def step(r, carry):
            left = jnp.concatenate([tb[inv[r, 0, c]] for c in cols], axis=1)
            prod = jnp.dot(left, right, preferred_element_type=F32).reshape(2, 2, OWN, HALF)
            zt, yt = r // (NY // 2), (r % (NY // 2)) * 2
            if not first:
                prod += acc[h, zt, pl.ds(yt, 2)]
            acc[h, zt, pl.ds(yt, 2)] = prod
            if last:
                pc[h, zt, pl.ds(yt, 2)] = prod.astype(BF)
            return carry

        lax.fori_loop(0, RT, step, 0, unroll=2)

    def group(h, dz, arrivals):
        arrivals.wait()
        forward_group(h, dz, dz == 0, dz == 1)

    def spread(h, d):
        own_z[h][d - 1].wait()
        return send_same(0, xs.at[h, slot(-d, 0)], x_peers)

    def to_partner_core(h):
        return send_all(0, [pc.at[h, :, :, 1 - co]], [rc.at[h]], [other])

    def add_partner_core(h, copy):
        copy.wait()
        s[h] = (acc[h, :, :, co] + rc[h].astype(F32)).astype(BF)

    def transpose_body(c, carry):
        for k in range(SLOTS):
            tT[c, :, k * TILE:(k + 1) * TILE] = tb[c * SLOTS + k].T
        return carry

    group(0, 0, own_x[0])
    near = [[None] * ZH, [None] * ZH]
    for d in range(1, ZH):
        near[0][ZH - d] = spread(0, d)
    group(1, 0, own_x[1])
    for d in range(1, ZH):
        near[1][ZH - d] = spread(1, d)
    for d in range(1, ZH):
        group(0, ZH - d, near[0][ZH - d])
    core0 = to_partner_core(0)
    for d in range(1, ZH):
        group(1, ZH - d, near[1][ZH - d])
    core1 = to_partner_core(1)
    add_partner_core(0, core0)
    y0 = send_all(0, [s.at[0, :, off(y, d, NY)] for d in range(1, NY)], [ry0.at[d] for d in range(1, NY)], y_peers)
    add_partner_core(1, core1)
    z1 = send_all(0, [s.at[1, off(zl, d, ZL)] for d in range(1, ZL)], [rz1.at[d] for d in range(1, ZL)], zl_peers)
    lax.fori_loop(0, NC, transpose_body, 0)
    for copy in load_rest:
        copy.wait()

    def add_up(total, ref):
        for d in range(1, ref.shape[0]):
            total += ref[d].astype(F32)
        return total

    z1.wait()
    t1[...] = add_up(s[1, zl].astype(F32), rz1).astype(BF)
    y1 = send_all(0, [t1.at[off(y, d, NY)] for d in range(1, NY)], [ry1.at[d] for d in range(1, NY)], y_peers)
    y0.wait()
    t0[...] = add_up(s[0, :, y].astype(F32), ry0).astype(BF)
    z0 = send_all(0, [t0.at[off(zl, d, ZL)] for d in range(1, ZL)], [rz0.at[d] for d in range(1, ZL)], zl_peers)
    y1.wait()
    ax1 = add_up(t1[y].astype(F32), ry1)
    z0.wait()
    ax0 = add_up(t0[zl].astype(F32), rz0)

    ax = jnp.concatenate([ax0, ax1], axis=1)
    high = ax.astype(BF)
    low = (ax - high.astype(F32)).astype(BF)
    w = wv[...]
    pre = jnp.dot(high, w, preferred_element_type=F32) + jnp.dot(low, w, preferred_element_type=F32)
    sig = jax.nn.sigmoid(pre)
    grad = (gout[...].astype(F32) * sig * (1.0 + pre * (1.0 - sig))).astype(BF)
    back = lax.dot_general(grad, w, (((1,), (1,)), ((), ())), preferred_element_type=F32).astype(BF)
    gg0[zl, y, co] = back[:, :HALF]
    gg1[zl, y, co] = back[:, HALF:]

    a0 = send_same(1, gg0.at[zl, y, co], zl_peers)
    a1 = send_same(1, gg1.at[zl, y, co], y_peers)
    out[...] = (pre * sig).astype(BF)

    gw1s[...] = lax.dot_general(
        jnp.concatenate([high, low], axis=0), jnp.concatenate([grad, grad], axis=0),
        (((0,), (0,)), ((), ())), preferred_element_type=F32,
    ).reshape(2, TILE, 2 * HALF)
    g1 = send_all(1, [gw1s.at[1 - co]], [gw1], [other])
    g1.wait()
    gw2s[...] = (gw1s[co] + gw1[...]).reshape(NY, OWN // 2, 2 * HALF).astype(BF)
    g2 = send_all(1, [gw2s.at[off(y, d, NY)] for d in range(1, NY)], [gw2.at[d] for d in range(1, NY)], y_peers)

    a0.wait()
    line = gg0.at[pl.ds(0, ZL), y, co]
    b0 = [send_all(1, [line], [line], [device]) for device in y_peers]
    c0 = send_same(1, line, [other])
    a1.wait()
    line = gg1.at[zl, :, co]
    b1 = [send_all(1, [line], [line], [device]) for device in zl_peers]
    c1 = send_same(1, line, [other])
    g2.wait()
    gw3[zl] = add_up(gw2s[y].astype(F32), gw2)
    g3 = send_same(1, gw3.at[zl], zl_peers)
    for d in range(1, ZL):
        b1[d - 1].wait()
        line = gg1.at[off(zl, -d, ZL), :, co]
        c1.send(line, line, other)
    g3.wait()
    gw4[x] = (gw3[0] + gw3[1]) + (gw3[2] + gw3[3])
    g4 = send_same(1, gw4.at[x], x_peers)
    for d in range(1, NY):
        b0[d - 1].wait()
        line = gg0.at[pl.ds(0, ZL), off(y, -d, NY), co]
        c0.send(line, line, other)

    def back_term(h, dz, dx):
        ref = (gg0, gg1)[h]
        c = slot(dz, dx)
        picks = []
        for k in range(SLOTS):
            r = ridx[k, 0, c]
            picks.append(ref[r >> 2, pl.ds((r & 3) * 2, 2)].reshape(TILE, HALF))
        return jnp.dot(tT[c], jnp.concatenate(picks, axis=0), preferred_element_type=F32)

    sx = {}

    def products(h, low, count):
        base = len(groups)
        for dz in range(low, low + count):
            sx[h, dz] = Group(1)
            sx[h, dz].count((NX - 1) * size(part.at[h, dz, 0]))

        def step(i, carry):
            dz, dx = low + i // (NX - 1), 1 + i % (NX - 1)
            part[h, dz, dx] = back_term(h, dz, dx).astype(BF)
            remote(part.at[h, dz, dx], fx.at[h, dz, dx], base + i // (NX - 1), 1, at(x_=off(x, dx, NX))).start()
            return carry

        lax.fori_loop(0, count * (NX - 1), step, 0)

    def own_products(h):
        def step(dz, carry):
            own[h, dz] = back_term(h, dz, 0)
            return carry

        lax.fori_loop(0, ZH, step, 0)

    def total_over_x(h, dz):
        sx[h, dz].wait()
        return add_up(own[h, dz], fx.at[h, dz])

    sz = {}

    def to_z(h, dz):
        fs[h, dz - 1] = total_over_x(h, dz).astype(BF)
        sz[h, dz] = send_all(1, [fs.at[h, dz - 1]], [fz.at[h, dz - 1]], [zh_peers[dz - 1]])

    def finish(h):
        term = own[h, 0]
        for dz in range(1, ZH):
            sz[h, dz].wait()
            term += fz[h, dz - 1].astype(F32)
        gfeat[:, h * HALF:(h + 1) * HALF] = term.astype(BF)

    c1.wait()
    products(1, 1, 2)
    g4.wait()
    gw5[zh] = (gw4[0] + gw4[1]) + (gw4[2] + gw4[3])
    g5 = send_same(1, gw5.at[zh], zh_peers)
    c0.wait()
    products(0, 1, 2)
    own_products(1)
    for dz in range(1, ZH):
        to_z(1, dz)
    own_products(0)
    for dz in range(1, ZH):
        to_z(0, dz)
    products(1, 0, 1)
    products(0, 0, 1)
    g5.wait()
    gwa[co, y] = (gw5[0] + gw5[1] + gw5[2]).astype(BF)
    g6 = send_same(1, gwa.at[co, y], y_peers)
    for h in (1, 0):
        own[h, 0] = total_over_x(h, 0)
    finish(1)
    g6.wait()
    g7 = send_same(1, gwa.at[co], [other])
    finish(0)
    g7.wait()
    gweight[...] = gwa[...].reshape(2 * HALF, 2 * HALF).astype(F32)
    for phase in range(2):
        ref = spare.at[pl.ds(0, sent[phase])]
        remote(ref, ref, 0, phase, other).wait_send()


def body(features, weight, tile_values, tile_rows, tile_counts, grad_out):
    vmem = pl.BlockSpec(memory_space=pltpu.VMEM)
    hbm = pl.BlockSpec(memory_space=pltpu.HBM)
    rows16 = OWN // 2
    return pl.pallas_call(
        kernel,
        out_shape=(
            jax.ShapeDtypeStruct(grad_out.shape, BF),
            jax.ShapeDtypeStruct(features.shape, BF),
            jax.ShapeDtypeStruct(weight.shape, F32),
        ),
        in_specs=[hbm] * 6,
        out_specs=(vmem, vmem, vmem),
        scratch_shapes=[
            pltpu.VMEM((NTILES + 1, TILE, TILE), BF),
            pltpu.VMEM((NC, TILE, SLOTS * TILE), BF),
            pltpu.VMEM(weight.shape, BF),
            pltpu.VMEM(grad_out.shape, BF),
            pltpu.VMEM((SLOTS, 1, NC), jnp.int32),
            pltpu.VMEM((1, NC), jnp.int32),
            pltpu.VMEM((RT, 1, NC), jnp.int32),
            pltpu.VMEM((SLOTS, 1, NC), jnp.int32),
            pltpu.SMEM((RT, 1, NC), jnp.int32),
            pltpu.SMEM((SLOTS, 1, NC), jnp.int32),
            pltpu.VMEM((2, NC, TILE, HALF), BF),
            pltpu.VMEM((2, ZL, NY, 2, OWN, HALF), F32),
            pltpu.VMEM((2, ZL, NY, 2, OWN, HALF), BF),
            pltpu.VMEM((2, ZL, NY, OWN, HALF), BF),
            pltpu.VMEM((2, ZL, NY, OWN, HALF), BF),
            pltpu.VMEM((NY, ZL, OWN, HALF), BF),
            pltpu.VMEM((ZL, OWN, HALF), BF),
            pltpu.VMEM((ZL, NY, OWN, HALF), BF),
            pltpu.VMEM((NY, OWN, HALF), BF),
            pltpu.VMEM((ZL, OWN, HALF), BF),
            pltpu.VMEM((NY, OWN, HALF), BF),
            pltpu.VMEM((ZL + 1, NY, 2, OWN, HALF), BF),
            pltpu.VMEM((ZL + 1, NY, 2, OWN, HALF), BF),
            pltpu.VMEM((2, ZH, NX, TILE, HALF), BF),
            pltpu.VMEM((2, ZH, NX, TILE, HALF), BF),
            pltpu.VMEM((2, ZH, TILE, HALF), F32),
            pltpu.VMEM((2, ZH - 1, TILE, HALF), BF),
            pltpu.VMEM((2, ZH - 1, TILE, HALF), BF),
            pltpu.VMEM((2, TILE, 2 * HALF), F32),
            pltpu.VMEM((TILE, 2 * HALF), F32),
            pltpu.VMEM((NY, rows16, 2 * HALF), BF),
            pltpu.VMEM((NY, rows16, 2 * HALF), BF),
            pltpu.VMEM((ZL, rows16, 2 * HALF), F32),
            pltpu.VMEM((NX, rows16, 2 * HALF), F32),
            pltpu.VMEM((ZH, rows16, 2 * HALF), F32),
            pltpu.VMEM((2, NY, rows16, 2 * HALF), BF),
            pltpu.VMEM((N_UNITS, OWN, HALF), BF),
            pltpu.SemaphoreType.DMA((9,)),
            pltpu.SemaphoreType.DMA((2,)),
            pltpu.SemaphoreType.DMA((N_GROUPS,)),
        ],
        compiler_params=pltpu.CompilerParams(
            collective_id=0, has_side_effects=True, vmem_limit_bytes=63 * 2 ** 20
        ),
    )(
        features, weight, tile_values.reshape(NTILES, TILE, TILE),
        tile_rows.transpose(3, 0, 1, 2).reshape(SLOTS, 1, NC), tile_counts.reshape(1, NC), grad_out,
    )


def solution(mesh):
    in_specs = (
        P(("blk", "team"), None),
        P(),
        P("blk", "team", None, None, None, None),
        P("blk", "team", None, None),
        P("blk", "team", None),
        P(("blk", "team"), None),
    )
    out_specs = (P(("blk", "team"), None), P(("blk", "team"), None), P())
    return jax.shard_map(body, mesh=mesh, in_specs=in_specs, out_specs=out_specs, check_vma=False)
```

time: 1370 us -> 86.8 us (0.06)
  waiting for transfers between devices: 1020 us -> 0 us
  loops' own time: 126 us -> 0 us
  Pallas kernels: 0 us -> 81.4 us
  starting transfers between devices: 66.5 us -> 0 us
  matrix products: 56.9 us -> 0 us
  other arithmetic: 49.8 us -> 0 us
  between operations: 25.3 us -> 0.64 us
  local copies, waits for them, and re-layouts: 24.3 us -> 4.46 us
    psum x1 -> x0, waiting for transfers between devices: 471 us -> none  [body(): grad_weight = lax.psum(local_weight, ('blk', 'team'))]
    reduce_scatter x1 -> x0, waiting for transfers between devices: 283 us -> none  [body(): lax.psum_scatter(partial_value.reshape(block_rows, width), 'team', scatte...]
    ppermute x22 -> x0, waiting for transfers between devices: 148 us -> none  [from_behind(): return lax.ppermute(block, axis, route)]
    another operation x2 -> x0, loops' own time: 126 us -> none  [the longest x1 126 us: body(): lax.fori_loop(1, blocks, forward_step, (hidden, forward_term(empty_full,...]
    all_gather x1 -> x0, waiting for transfers between devices: 117 us -> none  [body(): lax.all_gather(grad_pre, 'team', axis=0, tiled=True)]
    pallas_call x0 -> x1, Pallas kernels: none -> 81.4 us  [body(): pl.pallas_call(kernel, out_shape=(jax.ShapeDtypeStruct(grad_out.shape, BF...]
    ppermute x22 -> x0, starting transfers between devices: 66.4 us -> none  [from_behind(): return lax.ppermute(block, axis, route)]
    dot_general x39 -> x0, matrix products: 56.9 us -> none  [the longest x12 21.7 us: backward_term(): jnp.einsum('kij,kif->jf', tiles_c, chosen, preferred_element_type=jnp.flo...]
  transfers between devices with their start and end apart: 25 -> 0, of which waited for: 15 -> 0; matrix products, arithmetic and copies ran while one was open for 3% -> 0% of each run, Pallas kernels for 0% -> 0%
where the time goes in v2:
time: 86.8 us; the launch traced here: 86.5 us
  Pallas kernels  81.4 us (94%)
  local copies, waits for them, and re-layouts  4.46 us (5%)
    pallas_call x1, Pallas kernels, body(): pl.pallas_call(kernel, out_shape=(jax.ShapeDtypeStruct(grad_out.shape, BF...  81.4 us
    unnamed x3, local copies, waits for them, and re-layouts  4.46 us

profile of v2, /device:TPU:1, one launch (start us, length us, event | category | flops | bytes accessed | tf_op | source)
XLA Modules:
  0.0 86.5 jit_solution(18300251401894679662)
XLA Ops:
  0.6 81.4 %shard_map.85 = (bf16[32,256]{1,0:T(8,128)(2,1)}, bf16[128,256]{1,0:T(8,128)(2,1)}, f32[256,256]{1,0:T(8,128)}) custom-call(bf16[128,256]{1,0:T(8,128)(2,1)} %feat.1, bf16[256,256]{1,0:T(8,128)(2,1)} %weight.1, bf16[72,128,128]{2,1,0:T(8,128)(2,1)} %bitcast.5, s32[6,1,12]{2,1,0:T(1,128)} %bitcast.6, s32[1,12]{1,0:T(1,128)} %bitcast.7, bf16[32,256]{1,0:T(8,128)(2,1)} %gout_in.1), custom_call_target="tpu_custom_call" | custom-call | tf_op jit(solution)/shard_map/pallas_call | solution.py:335
  82.1 1.3 %copy.12 = bf16[32,256]{1,0:T(8,128)(2,1)} copy(bf16[32,256]{1,0:T(8,128)(2,1)} %get-tuple-element.6) | data formatting | bytes 32768
  83.4 1.5 %copy.13 = bf16[128,256]{1,0:T(8,128)(2,1)} copy(bf16[128,256]{1,0:T(8,128)(2,1)} %get-tuple-element.7) | data formatting | bytes 131072
  84.9 1.7 %copy.14 = f32[256,256]{1,0:T(8,128)} copy(f32[256,256]{1,0:T(8,128)} %get-tuple-element.8) | data formatting | bytes 524288

commit v3 on v2

--- a/solution.py
+++ b/solution.py
@@ -21,7 +21,7 @@
     feat, weight, tiles, rows_in, counts_in, gout_in,
     out, gfeat, gweight,
     tb, tT, wv, gout, rows, counts, inv_v, ridx_v, inv, ridx, xs, acc, pc, rc, s, ry0, rz0, rz1, ry1, t0, t1, gg0, gg1,
-    part, fx, own, fs, fz, gw1s, gw1, gw2s, gw2, gw3, gw4, gw5, gwa,
+    part, fx, own, fs, fz, gw1s, gw1, gw2s, gw2, gw3, gw4, gwa,
     spare, load_sem, send_sem, recv_sem,
 ):
     blk, team = lax.axis_index("blk"), lax.axis_index("team")
@@ -41,7 +41,9 @@
     zh_peers = [at(zh_=off(zh, d, ZH)) for d in range(1, ZH)]
 
     barrier = pltpu.get_barrier_semaphore()
-    partners = zh_peers + y_peers + x_peers + zl_peers + [other]
+    blk_peers = [(off(blk, d, NC), team) for d in range(1, NC)]
+    y_cross = [at(y_=off(y, d, NY), co_=1 - co) for d in range(1, NY)]
+    partners = blk_peers + y_peers + y_cross + zl_peers + [other]
     for device in partners:
         pl.semaphore_signal(barrier, inc=1, device_id=device, device_id_type=MESH)
 
@@ -59,7 +61,7 @@
     load_rest = [load(weight, wv), load(gout_in, gout)]
 
     unit = OWN * HALF * 2
-    groups, sent = [], [0, 0]
+    groups, sent = [], [0, 0, 0]
 
     def remote(src, dst, group, phase, device):
         return pltpu.make_async_remote_copy(
@@ -89,19 +91,26 @@
 
     def send_all(phase, sources, targets, devices):
         group = Group(phase)
-        for src, dst, device in zip(sources, targets, devices):
-            group.send(src, dst, device)
+        n = len(devices)
+        for i in sorted(range(n), key=lambda i: abs(2 * i - n + 1)):
+            group.send(sources[i], targets[i], devices[i])
         return group
 
     def send_same(phase, ref, devices):
         return send_all(phase, [ref] * len(devices), [ref] * len(devices), devices)
 
-    for copy in load_x:
-        copy.wait()
     pl.semaphore_wait(barrier, len(partners))
 
-    own_z = [[send_same(0, xs.at[h, blk], [device]) for device in zh_peers] for h in range(2)]
-    own_x = [send_same(0, xs.at[h, blk], x_peers) for h in range(2)]
+    def send_own(h, devices, phase=0):
+        block, target = feat.at[:, h * HALF:(h + 1) * HALF], xs.at[h, blk]
+        return send_all(phase, [block] * len(devices), [target] * len(devices), devices)
+
+    def wait_sent(phase):
+        ref = spare.at[pl.ds(0, sent[phase])]
+        remote(ref, ref, 0, phase, other).wait_send()
+
+    own_z = [[send_own(0, [device], 2) for device in zh_peers]]
+    own_x = [send_own(h, x_peers) for h in range(2)]
 
     tb[NTILES] = jnp.zeros((TILE, TILE), BF)
     for ref in (gg0, gg1):
@@ -113,13 +122,15 @@
     first_tile = lax.broadcasted_iota(jnp.int32, (1, NC), 1) * SLOTS
     rowof = [jnp.where(k < live, rows[k], RT) for k in range(SLOTS)]
     for k in range(SLOTS):
-        ridx_v[k] = rowof[k]
+        ridx_v[k] = jnp.where(rowof[k] == RT, RT, (rowof[k] - zl * (RT // ZL) + RT) & (RT - 1))
     for r in range(RT):
         found = jnp.full((1, NC), NTILES, jnp.int32)
         for k in range(SLOTS):
             found = jnp.where(rowof[k] == r, first_tile + k, found)
         inv_v[r] = found
     load_index = [load(inv_v, inv), load(ridx_v, ridx)]
+    wait_sent(2)
+    own_z.append([send_own(1, [device]) for device in zh_peers])
     for copy in load_index:
         copy.wait()
     load_tiles.wait()
@@ -127,33 +138,28 @@
     def slot(dz, dx):
         return off(zh, dz, ZH) * NX + off(x, dx, NX)
 
-    def forward_group(h, dz, first, last):
+    def forward_group(h, dz, low=0, high=RT // 2):
         cols = [slot(dz, dx) for dx in range(NX)]
         right = jnp.concatenate([xs[h, c] for c in cols], axis=0)
 
-        def step(r, carry):
-            left = jnp.concatenate([tb[inv[r, 0, c]] for c in cols], axis=1)
-            prod = jnp.dot(left, right, preferred_element_type=F32).reshape(2, 2, OWN, HALF)
-            zt, yt = r // (NY // 2), (r % (NY // 2)) * 2
-            if not first:
-                prod += acc[h, zt, pl.ds(yt, 2)]
-            acc[h, zt, pl.ds(yt, 2)] = prod
-            if last:
-                pc[h, zt, pl.ds(yt, 2)] = prod.astype(BF)
+        def step(i, carry):
+            left = jnp.concatenate(
+                [jnp.concatenate([tb[inv[2 * i + j, 0, c]] for c in cols], axis=1) for j in range(2)], axis=0
+            )
+            prod = jnp.dot(left, right, preferred_element_type=F32).reshape(4, 2, OWN, HALF)
+            zt, yt = i // (NY // 4), pl.ds((i % (NY // 4)) * 4, 4)
+            if dz:
+                prod += acc[h, zt, yt]
+            acc[h, zt, yt] = prod
+            if dz == 1:
+                pc[h, zt, yt] = prod.astype(BF)
             return carry
 
-        lax.fori_loop(0, RT, step, 0, unroll=2)
-
-    def group(h, dz, arrivals):
-        arrivals.wait()
-        forward_group(h, dz, dz == 0, dz == 1)
+        lax.fori_loop(low, high, step, 0)
 
     def spread(h, d):
         own_z[h][d - 1].wait()
         return send_same(0, xs.at[h, slot(-d, 0)], x_peers)
-
-    def to_partner_core(h):
-        return send_all(0, [pc.at[h, :, :, 1 - co]], [rc.at[h]], [other])
 
     def add_partner_core(h, copy):
         copy.wait()
@@ -164,22 +170,34 @@
             tT[c, :, k * TILE:(k + 1) * TILE] = tb[c * SLOTS + k].T
         return carry
 
-    group(0, 0, own_x[0])
+    for copy in load_x:
+        copy.wait()
     near = [[None] * ZH, [None] * ZH]
+    own_x[0].wait()
+    forward_group(0, 0)
     for d in range(1, ZH):
         near[0][ZH - d] = spread(0, d)
-    group(1, 0, own_x[1])
+    own_x[1].wait()
+    forward_group(1, 0)
     for d in range(1, ZH):
         near[1][ZH - d] = spread(1, d)
-    for d in range(1, ZH):
-        group(0, ZH - d, near[0][ZH - d])
-    core0 = to_partner_core(0)
-    for d in range(1, ZH):
-        group(1, ZH - d, near[1][ZH - d])
-    core1 = to_partner_core(1)
-    add_partner_core(0, core0)
+    core = [Group(0), Group(0)]
+
+    def finish_forward(h):
+        for dz in (2, 1):
+            near[h][dz].wait()
+            if dz == 2:
+                forward_group(h, dz)
+        for part_ in range(2):
+            forward_group(h, 1, part_ * RT // 4, (part_ + 1) * RT // 4)
+            rows_ = pl.ds(part_ * ZL // 2, ZL // 2)
+            core[h].send(pc.at[h, rows_, :, 1 - co], rc.at[h, rows_], other)
+
+    finish_forward(0)
+    add_partner_core(0, core[0])
     y0 = send_all(0, [s.at[0, :, off(y, d, NY)] for d in range(1, NY)], [ry0.at[d] for d in range(1, NY)], y_peers)
-    add_partner_core(1, core1)
+    finish_forward(1)
+    add_partner_core(1, core[1])
     z1 = send_all(0, [s.at[1, off(zl, d, ZL)] for d in range(1, ZL)], [rz1.at[d] for d in range(1, ZL)], zl_peers)
     lax.fori_loop(0, NC, transpose_body, 0)
     for copy in load_rest:
@@ -209,11 +227,18 @@
     sig = jax.nn.sigmoid(pre)
     grad = (gout[...].astype(F32) * sig * (1.0 + pre * (1.0 - sig))).astype(BF)
     back = lax.dot_general(grad, w, (((1,), (1,)), ((), ())), preferred_element_type=F32).astype(BF)
-    gg0[zl, y, co] = back[:, :HALF]
-    gg1[zl, y, co] = back[:, HALF:]
-
-    a0 = send_same(1, gg0.at[zl, y, co], zl_peers)
-    a1 = send_same(1, gg1.at[zl, y, co], y_peers)
+    gg0[0, y, co] = back[:, :HALF]
+    gg1[0, y, co] = back[:, HALF:]
+
+    def to_zl(ref, place):
+        group = Group(1)
+        for d in range(1, ZL):
+            group.send(ref.at[(0,) + place], ref.at[(ZL - d,) + place], zl_peers[d - 1])
+        return group
+
+    a0 = to_zl(gg0, (y, co))
+    a1 = send_same(1, gg1.at[0, y, co], y_peers)
+    b0 = [send_same(1, gg0.at[0, y, co], [device]) for device in y_peers]
     out[...] = (pre * sig).astype(BF)
 
     gw1s[...] = lax.dot_general(
@@ -226,27 +251,30 @@
     g2 = send_all(1, [gw2s.at[off(y, d, NY)] for d in range(1, NY)], [gw2.at[d] for d in range(1, NY)], y_peers)
 
     a0.wait()
+    line = gg0.at[pl.ds(1, ZL - 1), y, co]
+    by_distance = sorted(range(1, NY), key=lambda d: -min(d, NY - d))
+    for d in by_distance:
+        b0[d - 1].send(line, line, y_peers[d - 1])
     line = gg0.at[pl.ds(0, ZL), y, co]
-    b0 = [send_all(1, [line], [line], [device]) for device in y_peers]
     c0 = send_same(1, line, [other])
     a1.wait()
-    line = gg1.at[zl, :, co]
-    b1 = [send_all(1, [line], [line], [device]) for device in zl_peers]
+    line = gg1.at[0, :, co]
+    b1 = [send_all(1, [line], [gg1.at[ZL - d, :, co]], [zl_peers[d - 1]]) for d in range(1, ZL)]
     c1 = send_same(1, line, [other])
     g2.wait()
     gw3[zl] = add_up(gw2s[y].astype(F32), gw2)
     g3 = send_same(1, gw3.at[zl], zl_peers)
     for d in range(1, ZL):
         b1[d - 1].wait()
-        line = gg1.at[off(zl, -d, ZL), :, co]
+        line = gg1.at[ZL - d, :, co]
         c1.send(line, line, other)
-    g3.wait()
-    gw4[x] = (gw3[0] + gw3[1]) + (gw3[2] + gw3[3])
-    g4 = send_same(1, gw4.at[x], x_peers)
-    for d in range(1, NY):
+    for d in by_distance[::-1]:
         b0[d - 1].wait()
         line = gg0.at[pl.ds(0, ZL), off(y, -d, NY), co]
         c0.send(line, line, other)
+    g3.wait()
+    gw4[blk] = ((gw3[0] + gw3[1]) + (gw3[2] + gw3[3])).astype(BF)
+    g4 = send_same(1, gw4.at[blk], blk_peers)
 
     def back_term(h, dz, dx):
         ref = (gg0, gg1)[h]
@@ -266,7 +294,8 @@
             sx[h, dz].count((NX - 1) * size(part.at[h, dz, 0]))
 
         def step(i, carry):
-            dz, dx = low + i // (NX - 1), 1 + i % (NX - 1)
+            dz, j = low + i // (NX - 1), i % (NX - 1)
+            dx = 2 - j + 3 * (j // 2)
             part[h, dz, dx] = back_term(h, dz, dx).astype(BF)
             remote(part.at[h, dz, dx], fx.at[h, dz, dx], base + i // (NX - 1), 1, at(x_=off(x, dx, NX))).start()
             return carry
@@ -299,9 +328,6 @@
 
     c1.wait()
     products(1, 1, 2)
-    g4.wait()
-    gw5[zh] = (gw4[0] + gw4[1]) + (gw4[2] + gw4[3])
-    g5 = send_same(1, gw5.at[zh], zh_peers)
     c0.wait()
     products(0, 1, 2)
     own_products(1)
@@ -310,22 +336,22 @@
     own_products(0)
     for dz in range(1, ZH):
         to_z(0, dz)
+    g4.wait()
+    sub = gw4[0].astype(F32)
+    for c in range(1, NC):
+        sub += gw4[c].astype(F32)
+    gwa[co, y] = sub.astype(BF)
+    g5 = send_same(1, gwa.at[co, y], y_peers + y_cross + [other])
     products(1, 0, 1)
     products(0, 0, 1)
-    g5.wait()
-    gwa[co, y] = (gw5[0] + gw5[1] + gw5[2]).astype(BF)
-    g6 = send_same(1, gwa.at[co, y], y_peers)
     for h in (1, 0):
         own[h, 0] = total_over_x(h, 0)
     finish(1)
-    g6.wait()
-    g7 = send_same(1, gwa.at[co], [other])
     finish(0)
-    g7.wait()
+    g5.wait()
     gweight[...] = gwa[...].reshape(2 * HALF, 2 * HALF).astype(F32)
     for phase in range(2):
-        ref = spare.at[pl.ds(0, sent[phase])]
-        remote(ref, ref, 0, phase, other).wait_send()
+        wait_sent(phase)
 
 
 def body(features, weight, tile_values, tile_rows, tile_counts, grad_out):
@@ -335,9 +361,9 @@
     return pl.pallas_call(
         kernel,
         out_shape=(
-            jax.ShapeDtypeStruct(grad_out.shape, BF),
-            jax.ShapeDtypeStruct(features.shape, BF),
-            jax.ShapeDtypeStruct(weight.shape, F32),
+            pltpu.VMEM(grad_out.shape, BF),
+            pltpu.VMEM(features.shape, BF),
+            pltpu.VMEM(weight.shape, F32),
         ),
         in_specs=[hbm] * 6,
         out_specs=(vmem, vmem, vmem),
@@ -375,16 +401,15 @@
             pltpu.VMEM((NY, rows16, 2 * HALF), BF),
             pltpu.VMEM((NY, rows16, 2 * HALF), BF),
             pltpu.VMEM((ZL, rows16, 2 * HALF), F32),
-            pltpu.VMEM((NX, rows16, 2 * HALF), F32),
-            pltpu.VMEM((ZH, rows16, 2 * HALF), F32),
+            pltpu.VMEM((NC, rows16, 2 * HALF), BF),
             pltpu.VMEM((2, NY, rows16, 2 * HALF), BF),
             pltpu.VMEM((N_UNITS, OWN, HALF), BF),
             pltpu.SemaphoreType.DMA((9,)),
-            pltpu.SemaphoreType.DMA((2,)),
+            pltpu.SemaphoreType.DMA((3,)),
             pltpu.SemaphoreType.DMA((N_GROUPS,)),
         ],
         compiler_params=pltpu.CompilerParams(
-            collective_id=0, has_side_effects=True, vmem_limit_bytes=63 * 2 ** 20
+            collective_id=0, has_side_effects=True, vmem_limit_bytes=58 * 2 ** 20
         ),
     )(
         features, weight, tile_values.reshape(NTILES, TILE, TILE),

time: 86.8 us -> 81.6 us (0.940)
  Pallas kernels: 81.4 us -> 78.7 us
  local copies, waits for them, and re-layouts: 4.46 us -> 1.94 us
    pallas_call x1, Pallas kernels: 81.4 us -> 78.7 us  [body(): pl.pallas_call(kernel, out_shape=(pltpu.VMEM(grad_out.shape, BF), pltpu.V...]
    unnamed x3, local copies, waits for them, and re-layouts: 4.46 us -> 1.94 us
where the time goes in v3:
time: 81.6 us; the launch traced here: 81.3 us
  Pallas kernels  78.7 us (96%)
  local copies, waits for them, and re-layouts  1.94 us (2%)
    pallas_call x1, Pallas kernels, body(): pl.pallas_call(kernel, out_shape=(pltpu.VMEM(grad_out.shape, BF), pltpu.V...  78.7 us
    unnamed x3, local copies, waits for them, and re-layouts  1.94 us

profile of v3, /device:TPU:1, one launch (start us, length us, event | category | flops | bytes accessed | tf_op | source)
XLA Modules:
  0.0 81.3 jit_solution(14227809485168588585)
XLA Ops:
  0.6 78.7 %shard_map.85 = (bf16[32,256]{1,0:T(8,128)(2,1)S(1)}, bf16[128,256]{1,0:T(8,128)(2,1)S(1)}, f32[256,256]{1,0:T(8,128)S(1)}) custom-call(bf16[128,256]{1,0:T(8,128)(2,1)} %feat.1, bf16[256,256]{1,0:T(8,128)(2,1)} %weight.1, bf16[72,128,128]{2,1,0:T(8,128)(2,1)} %bitcast.5, s32[6,1,12]{2,1,0:T(1,128)} %bitcast.6, s32[1,12]{1,0:T(1,128)} %bitcast.7, ...), custom_call_target="tpu_custom_call" | custom-call | tf_op jit(solution)/shard_map/pallas_call | solution.py:361
  79.4 0.6 copy.12
  80.0 0.6 copy.13
  80.6 0.7 copy.14

commit v4 on v3

--- a/solution.py
+++ b/solution.py
@@ -138,8 +138,8 @@
     def slot(dz, dx):
         return off(zh, dz, ZH) * NX + off(x, dx, NX)
 
-    def forward_group(h, dz, low=0, high=RT // 2):
-        cols = [slot(dz, dx) for dx in range(NX)]
+    def forward_group(h, groups_, low=0, high=RT // 2):
+        cols = [slot(dz, dx) for dz in groups_ for dx in range(NX)]
         right = jnp.concatenate([xs[h, c] for c in cols], axis=0)
 
         def step(i, carry):
@@ -148,10 +148,10 @@
             )
             prod = jnp.dot(left, right, preferred_element_type=F32).reshape(4, 2, OWN, HALF)
             zt, yt = i // (NY // 4), pl.ds((i % (NY // 4)) * 4, 4)
-            if dz:
+            if 0 not in groups_:
                 prod += acc[h, zt, yt]
             acc[h, zt, yt] = prod
-            if dz == 1:
+            if 1 in groups_:
                 pc[h, zt, yt] = prod.astype(BF)
             return carry
 
@@ -174,29 +174,27 @@
         copy.wait()
     near = [[None] * ZH, [None] * ZH]
     own_x[0].wait()
-    forward_group(0, 0)
+    forward_group(0, (0,))
     for d in range(1, ZH):
         near[0][ZH - d] = spread(0, d)
     own_x[1].wait()
-    forward_group(1, 0)
+    forward_group(1, (0,))
     for d in range(1, ZH):
         near[1][ZH - d] = spread(1, d)
     core = [Group(0), Group(0)]
 
-    def finish_forward(h):
-        for dz in (2, 1):
-            near[h][dz].wait()
-            if dz == 2:
-                forward_group(h, dz)
+    def last_group(h):
+        near[h][2].wait()
+        near[h][1].wait()
         for part_ in range(2):
-            forward_group(h, 1, part_ * RT // 4, (part_ + 1) * RT // 4)
+            forward_group(h, (2, 1), part_ * RT // 4, (part_ + 1) * RT // 4)
             rows_ = pl.ds(part_ * ZL // 2, ZL // 2)
             core[h].send(pc.at[h, rows_, :, 1 - co], rc.at[h, rows_], other)
 
-    finish_forward(0)
+    last_group(0)
     add_partner_core(0, core[0])
     y0 = send_all(0, [s.at[0, :, off(y, d, NY)] for d in range(1, NY)], [ry0.at[d] for d in range(1, NY)], y_peers)
-    finish_forward(1)
+    last_group(1)
     add_partner_core(1, core[1])
     z1 = send_all(0, [s.at[1, off(zl, d, ZL)] for d in range(1, ZL)], [rz1.at[d] for d in range(1, ZL)], zl_peers)
     lax.fori_loop(0, NC, transpose_body, 0)

time: 81.6 us -> 81.6 us (level)
  no operation moved by 1% of the time
where the time goes in v4:
time: 81.6 us; the launch traced here: 81.4 us
  Pallas kernels  78.9 us (97%)
  local copies, waits for them, and re-layouts  1.94 us (2%)
    pallas_call x1, Pallas kernels, body(): pl.pallas_call(kernel, out_shape=(pltpu.VMEM(grad_out.shape, BF), pltpu.V...  78.9 us
    unnamed x3, local copies, waits for them, and re-layouts  1.94 us

profile of v4, /device:TPU:1, one launch (start us, length us, event | category | flops | bytes accessed | tf_op | source)
XLA Modules:
  0.0 81.4 jit_solution(9752627307614946545)
XLA Ops:
  0.6 78.9 %shard_map.85 = (bf16[32,256]{1,0:T(8,128)(2,1)S(1)}, bf16[128,256]{1,0:T(8,128)(2,1)S(1)}, f32[256,256]{1,0:T(8,128)S(1)}) custom-call(bf16[128,256]{1,0:T(8,128)(2,1)} %feat.1, bf16[256,256]{1,0:T(8,128)(2,1)} %weight.1, bf16[72,128,128]{2,1,0:T(8,128)(2,1)} %bitcast.5, s32[6,1,12]{2,1,0:T(1,128)} %bitcast.6, s32[1,12]{1,0:T(1,128)} %bitcast.7, ...), custom_call_target="tpu_custom_call" | custom-call | tf_op jit(solution)/shard_map/pallas_call | solution.py:359
  79.5 0.6 copy.12
  80.1 0.6 copy.13
  80.7 0.7 copy.14
